TPU v7x, 256 devices: a whole 4x4x8 slice. The times are simulated.
256 devices in a mesh: island: 8 (over y_hi, x), fsdp: 32 (over y_lo, z, core).
Axes of the slice: x: 4, y: 4 (y_hi: 2, y_lo: 2; y = y_hi * 2 + y_lo), z: 8, core: 2. Of those that a mesh axis runs over, the one named last changes fastest.
Arguments:
- hidden_in: bfloat16 [8, 8192, 8192], P('island', 'fsdp'), may hold values from -6 to 6
- norm_gain: bfloat16 [8, 8192], P('island'), may hold values from 0.5 to 2
- key_weight: bfloat16 [8, 8192, 512], P('island', 'fsdp'), may hold values from -0.0625 to 0.0625
- key_cotangent: bfloat16 [8, 8192, 512], P('island', 'fsdp'), may hold values from -6 to 6
- frag_global: float32 [8192, 512], P('fsdp'), may hold values from -6 to 6
- frag_moment: float32 [8192, 512], P('fsdp'), may hold values from -4 to 4
- frag_local: bfloat16 [8, 8192, 512], P('island', 'fsdp'), may hold values from -6 to 6
Outputs:
- keys: bfloat16 [8, 8192, 512], P('island', 'fsdp')
- grad_in: bfloat16 [8, 8192, 8192], P('island', 'fsdp')
- grad_w: float32 [8, 8192, 512], P('island', 'fsdp')
- new_global: float32 [8192, 512], P('fsdp')
- new_moment: float32 [8192, 512], P('fsdp')
- new_local: bfloat16 [8, 8192, 512], P('island', 'fsdp')
All inputs are finite; a program needn't handle non-finite values.
Results may differ from a plain program's by a relative error of at most 0.0049.
Values may be sent and summed in bfloat16 or wider, within the bound.
A program may use at most 128 MiB of HBM per device.

v0:
```python
import jax
import jax.numpy as jnp
from jax import lax
from jax.sharding import PartitionSpec as P

epsilon = 1e-05
outer_rate = 0.7
outer_momentum = 0.9
mix_weight = 0.5


def nesterov(pseudo, moment, params):
    new_moment = outer_momentum * moment + pseudo
    new_params = params - outer_rate * (pseudo + outer_momentum * new_moment)
    return (new_moment, new_params)


def body(hidden_in, norm_gain, key_weight, key_cotangent, frag_global, frag_moment, frag_local):
    hidden_f = hidden_in[0].astype(jnp.float32)
    gain_f = norm_gain[0].astype(jnp.float32)
    scale = lax.rsqrt(jnp.mean(hidden_f * hidden_f, axis=-1, keepdims=True) + epsilon)
    normed = (hidden_f * scale * gain_f).astype(jnp.bfloat16)
    cotangent = key_cotangent[0]
    gathered = lax.all_gather(key_weight, "fsdp", axis=1, tiled=True)[0]
    key_sum = jnp.dot(normed, gathered, preferred_element_type=jnp.float32)
    back = jnp.einsum("tk,dk->td", cotangent, gathered, preferred_element_type=jnp.float32)
    keys = key_sum.astype(jnp.bfloat16)
    upper = back * gain_f
    inner = jnp.mean(upper * hidden_f, axis=-1, keepdims=True)
    grad_in = (scale * upper - hidden_f * scale * scale * scale * inner).astype(jnp.bfloat16)
    grad_w = lax.psum_scatter(
        jnp.einsum("td,tk->dk", normed, cotangent, preferred_element_type=jnp.float32),
        "fsdp",
        scatter_dimension=0,
        tiled=True,
    )
    islands = lax.axis_size("island")
    local_f = frag_local[0].astype(jnp.float32)
    difference = frag_global - local_f
    summed = lax.psum(difference, "island")
    new_moment, new_global = nesterov(summed / islands, frag_moment, frag_global)
    new_local = (mix_weight * local_f + (1.0 - mix_weight) * new_global).astype(jnp.bfloat16)
    return (keys[None], grad_in[None], grad_w[None], new_global, new_moment, new_local[None])


def solution(mesh):
    in_specs = (
        P("island", "fsdp", None),
        P("island", None),
        P("island", "fsdp", None),
        P("island", "fsdp", None),
        P("fsdp", None),
        P("fsdp", None),
        P("island", "fsdp", None),
    )
    out_specs = (
        P("island", "fsdp", None),
        P("island", "fsdp", None),
        P("island", "fsdp", None),
        P("fsdp", None),
        P("fsdp", None),
        P("island", "fsdp", None),
    )
    return jax.shard_map(body, mesh=mesh, in_specs=in_specs, out_specs=out_specs, check_vma=False)
```

profile of v0, /device:TPU:2, one launch (start us, length us, event | category | flops | bytes accessed | tf_op | source)
XLA Modules:
  0.0 257.9 jit_solution(416443387016718516)
XLA Ops:
  8.0 0.0 copy-start
  8.0 0.0 all-gather.2.cloned.1.call-start
  8.1 0.7 all-gather.2.cloned.1.call-update
  8.7 0.0 all-reduce.2.cloned.1.call-start
  8.8 2.0 convert_subtract_fusion
  10.8 0.0 all-reduce.2.cloned.1.call-update
  10.8 0.0 reduce-scatter.2.cloned.1.call-start
  10.8 0.8 mul.110
  11.6 74.3 %all-gather.2.cloned.1.call-done = bf16[1,8192,512]{2,1,0:T(8,128)(2,1)} async-done(((bf16[1,256,512]{2,1,0:T(8,128)(2,1)}), bf16[1,8192,512]{2,1,0:T(8,128)(2,1)}) %all-gather.2.cloned.1.call-update) | async-done | bytes 8388624 | tf_op jit(solution)/shard_map/all_gather | solution.py:24
  86.0 0.0 copy-done
  86.0 11.9 %fusion.9 = (f32[256]{0:T(256)S(1)}, f32[256]{0:T(256)S(1)}, f32[256,8192]{1,0:T(8,128)}) fusion(bf16[1,256,8192]{2,1,0:T(8,128)(2,1)} %param.7, f32[8192]{0:T(1024)S(1)} %bitcast.62, bf16[1,8192,512]{2,1,0:T(8,128)(2,1)} %all-gather.2.cloned.1.call-done, bf16[1,256,512]{2,1,0:T(8,128)(2,1)S(1)} %copy-done), kind=kOutput, calls=%fused_computation.12 | convolution fusion | flops 2160066048 | bytes 21268480 | tf_op jit(solution)/shard_map/tk,dk->td/dot_general | solution.py:26
  97.9 0.0 copy-done.1
  97.9 8.3 %fusion.20 = f32[8192,512]{1,0:T(8,128)} fusion(bf16[1,256,8192]{2,1,0:T(8,128)(2,1)S(1)} %copy-done.1, f32[8192]{0:T(1024)S(1)} %bitcast.63, f32[256]{0:T(256)S(1)} %add_rsqrt_fusion, bf16[1,256,512]{2,1,0:T(8,128)(2,1)S(1)} %copy-done), kind=kOutput, calls=%fused_computation.21 | convolution fusion | flops 2155872256 | bytes 21267456 | tf_op jit(solution)/shard_map/td,tk->dk/dot_general | solution.py:32
  106.2 0.0 reduce-scatter.2.cloned.1.call-update
  106.2 0.0 all-reduce.2.cloned.1.call-done
  106.3 1.0 copy-done.3
  107.3 0.1 copy-done.4
  107.3 0.2 copy-done.5
  107.5 2.4 fusion.30
  109.9 7.9 %fusion.23 = bf16[1,256,512]{2,1,0:T(8,128)(2,1)} fusion(bf16[1,8192,512]{2,1,0:T(8,128)(2,1)} %all-gather.2.cloned.1.call-done, bf16[1,256,8192]{2,1,0:T(8,128)(2,1)} %param.7, f32[8192]{0:T(1024)S(1)} %bitcast.64, f32[256]{0:T(256)S(1)} %add_rsqrt_fusion), kind=kOutput, calls=%fused_computation.22 | convolution fusion | flops 2156003328 | bytes 12878848 | tf_op jit(solution)/shard_map/dot_general | solution.py:25
  117.8 0.0 slice-done
  117.8 0.0 copy-done.2
  117.8 3.7 %fusion.16 = bf16[1,256,8192]{2,1,0:T(8,128)(2,1)} fusion(bf16[1,256,8192]{2,1,0:T(8,128)(2,1)S(1)} %copy-done.2, f32[256,8192]{1,0:T(8,128)S(1)} %bitcast.61, f32[256]{0:T(256)S(1)} %broadcast_multiply_fusion, f32[256]{0:T(256)S(1)} %add_rsqrt_fusion), kind=kLoop, calls=%fused_computation.19 | loop fusion | flops 16777216 | bytes 16779264 | tf_op jit(solution)/shard_map/broadcast_in_dim | solution.py:43
  121.6 128.9 %reduce-scatter.2.cloned.1.call-done = f32[256,512]{1,0:T(8,128)} async-done(((f32[8192,512]{1,0:T(8,128)}), f32[256,512]{1,0:T(8,128)}) %reduce-scatter.2.cloned.1.call-update) | async-done | bytes 524304 | tf_op jit(solution)/shard_map/reduce_scatter | solution.py:31
  (11 shorter events, 0.0 us)
Async XLA Ops:
  8.0 78.0 %copy-start = (bf16[1,256,512]{2,1,0:T(8,128)(2,1)S(1)}, bf16[1,256,512]{2,1,0:T(8,128)(2,1)}, u32[]{:S(2)}) copy-start(bf16[1,256,512]{2,1,0:T(8,128)(2,1)} %param.10) | copy-start | bytes 786436
  8.0 78.0 %all-gather.2.cloned.1.call-start = ((), (), s32[]{:S(2)}) async-start(), calls=%async_computation.1 | async-start | bytes 8650752 | tf_op jit(solution)/shard_map/all_gather | solution.py:24
  8.7 97.5 %all-reduce.2.cloned.1.call-start = ((), (), s32[]{:S(2)}) async-start(), calls=%async_computation.3 | async-start | bytes 1048576 | tf_op jit(solution)/shard_map/psum | solution.py:40
  10.8 239.6 %reduce-scatter.2.cloned.1.call-start = ((), (), s32[]{:S(2)}) async-start(), calls=%async_computation.2 | async-start | bytes 17301504 | tf_op jit(solution)/shard_map/reduce_scatter | solution.py:31
  86.0 12.0 %copy-start.1 = (bf16[1,256,8192]{2,1,0:T(8,128)(2,1)S(1)}, bf16[1,256,8192]{2,1,0:T(8,128)(2,1)}, u32[]{:S(2)}) copy-start(bf16[1,256,8192]{2,1,0:T(8,128)(2,1)} %param.7) | copy-start | bytes 12582916
  106.2 1.0 copy-start.3
  106.2 1.1 copy-start.4
  106.2 1.3 copy-start.5
  107.5 10.3 %slice-start = ((s8[8388608]{0:T(1024)(128)(4,1)}), s8[4194304]{0:T(1024)(128)(4,1)S(1)}, s32[]{:S(2)}) async-start(s8[8388608]{0:T(1024)(128)(4,1)} %bitcast.60), calls=%async_computation.4 | async-start | bytes 8388608
  109.9 7.9 %copy-start.2 = (bf16[1,256,8192]{2,1,0:T(8,128)(2,1)S(1)}, bf16[1,256,8192]{2,1,0:T(8,128)(2,1)}, u32[]{:S(2)}) copy-start(bf16[1,256,8192]{2,1,0:T(8,128)(2,1)} %param.7) | copy-start | bytes 12582916
  109.9 7.9 %slice-start.1 = ((s8[8388608]{0:T(1024)(128)(4,1)}), s8[4194304]{0:T(1024)(128)(4,1)S(1)}, s32[]{:S(2)}) async-start(s8[8388608]{0:T(1024)(128)(4,1)} %bitcast.60), calls=%async_computation.5 | async-start | bytes 8388608
Sparse Core Ops, SparseCore 0:
  10.7 75.2 all-gather.1
  106.4 144.0 reduce-scatter.1
Sparse Core Ops, SparseCore 1:
  12.4 89.9 all-reduce.1
where the time goes:
time: 258 us
  waiting for transfers between devices  204 us (79%)
  matrix products  28.1 us (11%)
  between operations  15.5 us (6%)
  other arithmetic  8.93 us (3%)
    reduce_scatter x1, waiting for transfers between devices, body(): lax.psum_scatter(jnp.einsum('td,tk->dk', normed, cotangent, preferred_ele...  129 us
    all_gather x1, waiting for transfers between devices, body(): gathered = lax.all_gather(key_weight, 'fsdp', axis=1, tiled=True)[0]  74.3 us
    dot_general x1, matrix products, body(): jnp.einsum('tk,dk->td', cotangent, gathered, preferred_element_type=jnp.f...  11.9 us
    dot_general x1, matrix products, body(): jnp.einsum('td,tk->dk', normed, cotangent, preferred_element_type=jnp.flo...  8.27 us
    dot_general x1, matrix products, body(): key_sum = jnp.dot(normed, gathered, preferred_element_type=jnp.float32)  7.88 us
  transfers between devices with their start and end apart: 3, of which 2 were waited for; matrix products, arithmetic and copies ran while one was open for 14% of the time, Pallas kernels for 0%

commit v1 on v0

--- a/solution.py
+++ b/solution.py
@@ -1,3 +1,4 @@
+import functools
 import jax
 import jax.numpy as jnp
 from jax import lax
@@ -7,6 +8,16 @@
 outer_rate = 0.7
 outer_momentum = 0.9
 mix_weight = 0.5
+
+
+def serve_matrix(frame, named_axis, d_out):
+    lanes = []
+    for _ in range(lax.psum(1, named_axis)):
+        lanes.append(frame)
+    return jnp.concatenate(lax.all_to_all(jnp.stack(lanes), named_axis, 0, 0), axis=d_out)
+
+
+hubs_mark = functools.partial(serve_matrix, named_axis="fsdp", d_out=1)
 
 
 def nesterov(pseudo, moment, params):
@@ -21,7 +32,7 @@
     scale = lax.rsqrt(jnp.mean(hidden_f * hidden_f, axis=-1, keepdims=True) + epsilon)
     normed = (hidden_f * scale * gain_f).astype(jnp.bfloat16)
     cotangent = key_cotangent[0]
-    gathered = lax.all_gather(key_weight, "fsdp", axis=1, tiled=True)[0]
+    gathered = hubs_mark(key_weight)[0]
     key_sum = jnp.dot(normed, gathered, preferred_element_type=jnp.float32)
     back = jnp.einsum("tk,dk->td", cotangent, gathered, preferred_element_type=jnp.float32)
     keys = key_sum.astype(jnp.bfloat16)

time: 258 us -> 385 us (1.49)
  waiting for transfers between devices: 204 us -> 317 us
  starting transfers between devices: 0.12 us -> 10.2 us
  local copies, waits for them, and re-layouts: 1.24 us -> 6.19 us
    all_to_all x0 -> x1, waiting for transfers between devices: none -> 185 us  [serve_matrix(): lax.all_to_all(jnp.stack(lanes), named_axis, 0, 0)]
    all_gather x1 -> x0, waiting for transfers between devices: 74.3 us -> none  [body(): gathered = lax.all_gather(key_weight, 'fsdp', axis=1, tiled=True)[0]]
    all_to_all x0 -> x1, starting transfers between devices: none -> 10.1 us  [serve_matrix(): lax.all_to_all(jnp.stack(lanes), named_axis, 0, 0)]
    another operation x0 -> x1, local copies, waits for them, and re-layouts: none -> 5.17 us  [serve_matrix(): jnp.stack(lanes)]
  transfers between devices with their start and end apart: 3 -> 3, of which waited for: 2 -> 2; matrix products, arithmetic and copies ran while one was open for 14% -> 9% of each run, Pallas kernels for 0% -> 0%
where the time goes in v1:
time: 385 us; the launch traced here: 384 us
  waiting for transfers between devices  317 us (82%)
  matrix products  28.1 us (7%)
  between operations  15.6 us (4%)
  starting transfers between devices  10.2 us (3%)
  other arithmetic  7.06 us (2%)
  local copies, waits for them, and re-layouts  6.19 us (2%)
    all_to_all x1, waiting for transfers between devices, serve_matrix(): lax.all_to_all(jnp.stack(lanes), named_axis, 0, 0)  185 us
    reduce_scatter x1, waiting for transfers between devices, body(): lax.psum_scatter(jnp.einsum('td,tk->dk', normed, cotangent, preferred_ele...  132 us
    dot_general x1, matrix products, body(): jnp.einsum('tk,dk->td', cotangent, gathered, preferred_element_type=jnp.f...  11.9 us
    all_to_all x1, starting transfers between devices, serve_matrix(): lax.all_to_all(jnp.stack(lanes), named_axis, 0, 0)  10.1 us
    dot_general x1, matrix products, body(): jnp.einsum('td,tk->dk', normed, cotangent, preferred_element_type=jnp.flo...  8.27 us
    dot_general x1, matrix products, body(): key_sum = jnp.dot(normed, gathered, preferred_element_type=jnp.float32)  7.88 us
  transfers between devices with their start and end apart: 3, of which 2 were waited for; matrix products, arithmetic and copies ran while one was open for 9% of the time, Pallas kernels for 0%

profile of v1, /device:TPU:2, one launch (start us, length us, event | category | flops | bytes accessed | tf_op | source)
XLA Modules:
  0.0 384.4 jit_solution(15409244983341434424)
XLA Ops:
  8.0 0.0 copy-start
  8.0 5.2 %stack.2 = bf16[32,1,256,512]{3,2,1,0:T(8,128)(2,1)} broadcast(bf16[256,512]{1,0:T(8,128)(2,1)} %bitcast.55), dimensions={2,3} | broadcast | bytes 8650752 | tf_op jit(solution)/shard_map/stack | solution.py:17
  13.2 10.1 %all-to-all-start = ((bf16[32,1,256,512]{3,2,1,0:T(8,128)(2,1)}), bf16[32,1,256,512]{3,2,1,0:T(8,128)(2,1)}, u32[]{:S(2)}, u32[]{:S(2)}) async-start(bf16[32,1,256,512]{3,2,1,0:T(8,128)(2,1)} %stack.2), calls=%async_computation | async-start | bytes 16777216 | tf_op jit(solution)/shard_map/all_to_all | solution.py:17
  23.3 0.0 all-reduce.2.cloned.1.call-start
  23.4 0.0 copy-done.3
  23.4 0.0 copy-done.4
  23.4 0.9 convert_subtract_fusion
  24.3 0.0 all-reduce.2.cloned.1.call-update
  24.3 0.0 reduce-scatter.2.cloned.1.call-start
  24.3 0.0 copy-done.6
  24.4 185.1 %all-to-all-done = bf16[32,1,256,512]{3,2,1,0:T(8,128)(2,1)} async-done(((bf16[32,1,256,512]{3,2,1,0:T(8,128)(2,1)}), bf16[32,1,256,512]{3,2,1,0:T(8,128)(2,1)}, u32[]{:S(2)}, u32[]{:S(2)}) %all-to-all-start) | async-done | bytes 8388640 | tf_op jit(solution)/shard_map/all_to_all | solution.py:17
  209.5 0.0 copy-done
  209.5 11.9 %fusion.9 = (f32[256]{0:T(256)S(1)}, f32[256]{0:T(256)S(1)}, f32[256,8192]{1,0:T(8,128)}) fusion(bf16[1,256,8192]{2,1,0:T(8,128)(2,1)} %param.7, f32[8192]{0:T(1024)S(1)} %bitcast.56, bf16[8192,512]{1,0:T(8,128)(2,1)} %bitcast.4, bf16[1,256,512]{2,1,0:T(8,128)(2,1)S(1)} %copy-done), kind=kOutput, calls=%fused_computation.12 | convolution fusion | flops 2160066048 | bytes 21268480 | tf_op jit(solution)/shard_map/tk,dk->td/dot_general | solution.py:37
  221.4 0.0 copy-done.1
  221.4 8.3 %fusion.14 = f32[8192,512]{1,0:T(8,128)} fusion(bf16[1,256,8192]{2,1,0:T(8,128)(2,1)S(1)} %copy-done.1, f32[8192]{0:T(1024)S(1)} %bitcast.57, f32[256]{0:T(256)S(1)} %add_rsqrt_fusion, bf16[1,256,512]{2,1,0:T(8,128)(2,1)S(1)} %copy-done), kind=kOutput, calls=%fused_computation.18 | convolution fusion | flops 2155872256 | bytes 21267456 | tf_op jit(solution)/shard_map/td,tk->dk/dot_general | solution.py:43
  229.7 0.0 reduce-scatter.2.cloned.1.call-update
  229.7 0.0 all-reduce.2.cloned.1.call-done
  229.7 1.0 copy-done.5
  230.7 2.4 fusion.22
  233.2 7.9 %fusion.17 = bf16[1,256,512]{2,1,0:T(8,128)(2,1)} fusion(bf16[8192,512]{1,0:T(8,128)(2,1)} %bitcast.4, bf16[1,256,8192]{2,1,0:T(8,128)(2,1)} %param.7, f32[8192]{0:T(1024)S(1)} %bitcast.58, f32[256]{0:T(256)S(1)} %add_rsqrt_fusion), kind=kOutput, calls=%fused_computation.19 | convolution fusion | flops 2156003328 | bytes 12878848 | tf_op jit(solution)/shard_map/dot_general | solution.py:36
  241.1 0.0 slice-done
  241.1 0.0 copy-done.2
  241.1 3.7 fusion.13
  244.8 132.2 %reduce-scatter.2.cloned.1.call-done = f32[256,512]{1,0:T(8,128)} async-done(((f32[8192,512]{1,0:T(8,128)}), f32[256,512]{1,0:T(8,128)}) %reduce-scatter.2.cloned.1.call-update) | async-done | bytes 524304 | tf_op jit(solution)/shard_map/reduce_scatter | solution.py:42
  (13 shorter events, 0.1 us)
Async XLA Ops:
  8.0 201.5 %copy-start = (bf16[1,256,512]{2,1,0:T(8,128)(2,1)S(1)}, bf16[1,256,512]{2,1,0:T(8,128)(2,1)}, u32[]{:S(2)}) copy-start(bf16[1,256,512]{2,1,0:T(8,128)(2,1)} %param.10) | copy-start | bytes 786436
  13.2 10.2 %copy-start.3 = (f32[256,512]{1,0:T(8,128)S(1)}, f32[256,512]{1,0:T(8,128)}, u32[]{:S(2)}) copy-start(f32[256,512]{1,0:T(8,128)} %param.11) | copy-start | bytes 1572868
  13.2 10.2 %copy-start.4 = (bf16[1,256,512]{2,1,0:T(8,128)(2,1)S(1)}, bf16[1,256,512]{2,1,0:T(8,128)(2,1)}, u32[]{:S(2)}) copy-start(bf16[1,256,512]{2,1,0:T(8,128)(2,1)} %param.13) | copy-start | bytes 786436
  13.2 11.2 %copy-start.6 = (bf16[1,8192]{1,0:T(2,128)(2,1)S(1)}, bf16[1,8192]{1,0:T(2,128)(2,1)}, u32[]{:S(2)}) copy-start(bf16[1,8192]{1,0:T(2,128)(2,1)} %param.8) | copy-start | bytes 49156
  13.2 196.3 %all-to-all-start = ((bf16[32,1,256,512]{3,2,1,0:T(8,128)(2,1)}), bf16[32,1,256,512]{3,2,1,0:T(8,128)(2,1)}, u32[]{:S(2)}, u32[]{:S(2)}) async-start(bf16[32,1,256,512]{3,2,1,0:T(8,128)(2,1)} %stack.2), calls=%async_computation | async-start | bytes 16777216 | tf_op jit(solution)/shard_map/all_to_all | solution.py:17
  23.3 206.4 %all-reduce.2.cloned.1.call-start = ((), (), s32[]{:S(2)}) async-start(), calls=%async_computation.3 | async-start | bytes 1048576 | tf_op jit(solution)/shard_map/psum | solution.py:51
  24.3 352.7 %reduce-scatter.2.cloned.1.call-start = ((), (), s32[]{:S(2)}) async-start(), calls=%async_computation.2 | async-start | bytes 17301504 | tf_op jit(solution)/shard_map/reduce_scatter | solution.py:42
  209.5 12.0 %copy-start.1 = (bf16[1,256,8192]{2,1,0:T(8,128)(2,1)S(1)}, bf16[1,256,8192]{2,1,0:T(8,128)(2,1)}, u32[]{:S(2)}) copy-start(bf16[1,256,8192]{2,1,0:T(8,128)(2,1)} %param.7) | copy-start | bytes 12582916
  229.7 1.0 copy-start.5
  230.7 10.3 %slice-start = ((s8[8388608]{0:T(1024)(128)(4,1)}), s8[4194304]{0:T(1024)(128)(4,1)S(1)}, s32[]{:S(2)}) async-start(s8[8388608]{0:T(1024)(128)(4,1)} %bitcast.53), calls=%async_computation.4 | async-start | bytes 8388608
  233.2 7.9 %copy-start.2 = (bf16[1,256,8192]{2,1,0:T(8,128)(2,1)S(1)}, bf16[1,256,8192]{2,1,0:T(8,128)(2,1)}, u32[]{:S(2)}) copy-start(bf16[1,256,8192]{2,1,0:T(8,128)(2,1)} %param.7) | copy-start | bytes 12582916
  233.2 7.9 %slice-start.1 = ((s8[8388608]{0:T(1024)(128)(4,1)}), s8[4194304]{0:T(1024)(128)(4,1)S(1)}, s32[]{:S(2)}) async-start(s8[8388608]{0:T(1024)(128)(4,1)} %bitcast.53), calls=%async_computation.5 | async-start | bytes 8388608
Sparse Core Ops, SparseCore 0:
  27.4 94.5 all-reduce.1
Sparse Core Ops, SparseCore 1:
  229.8 147.1 reduce-scatter.1
